TPU v7x, 128 devices: a whole 4x4x4 slice. The times are simulated.
128 devices in a mesh: row: 16 (over y, x), col: 8 (over z, core).
Axes of the slice: x: 4, y: 4, z: 4, core: 2. Of those that a mesh axis runs over, the one named last changes fastest.
Arguments:
- band_tiles: bfloat16 [16, 128, 256, 256], P('row', 'col'), may hold values from 0.0009994507 to 1
- band_cell: int32 [16, 128], P('row', 'col'), may hold values from 0 to 31, as said below
- band_count: int32 [16, 8], P('row', 'col'), may hold values from 1 to 16, as said below
- matrix_tiles: bfloat16 [16, 64, 256, 256], P('row', 'col'), may hold values from 7.390976e-05 to 0.07421875
- matrix_col: int32 [16, 64], P('row', 'col'), may hold values from 0 to 15
- matrix_live: int32 [16, 64], P('row', 'col'), may hold values 0 or 1
Outputs:
- reached: bfloat16 [8192, 32768], P('row', 'col')
- gained: float32 [], replicated
Inputs may be any that keep to these rules, and one draw needn't show every extreme that they name: The band_cell values of one device's 16 slots are distinct. `band_count`: among the 8 devices of one index of row, the live slots with slot number 16 // 2 or more number at most 8 in all.
All inputs are finite; a program needn't handle non-finite values. No bound on the sum of `matrix_live` on one device may be relied on, other than what follows from the above.
Results may differ from a plain program's by a relative error of at most 0.001.
Values may be sent and summed in bfloat16 or wider, within the bound.
A program may use at most 128 MiB of HBM per device.

v0:
```python
import jax
import jax.numpy as jnp
from jax import lax
from jax.sharding import Mesh
from jax.sharding import PartitionSpec as P

TILES = 128
BR = 2
COL = ("col_0", "col_1")
ROW = ("row_0", "row_1")
ROW_COL = ("row_0", "row_1", "col_0", "col_1")


def rows_for(lines, length):
    spare = -lines.shape[0] % length
    if not spare:
        return lines
    return jnp.concatenate([lines, jnp.zeros((spare, *lines.shape[1:]), lines.dtype)])


def sum_by_parts(shard, axis):
    lines = shard.reshape(-1, *shard.shape[1:][-1:])
    own = lax.psum_scatter(
        rows_for(lines, lax.axis_size(axis)), axis, scatter_dimension=0, tiled=True
    )
    whole = lax.all_gather(own, axis).reshape(-1, *lines.shape[1:])
    return lax.slice_in_dim(whole, 0, len(lines)).reshape(shard.shape)


def over_axes(shard, axes):
    for axis in axes:
        shard = lax.psum(shard, axis)
    return shard


def on_device(band_tiles, band_cell, band_count, matrix_tiles, matrix_col, matrix_live):
    slots_own = band_tiles.shape[1]
    tile = band_tiles.shape[-1]
    n_col = lax.axis_size(COL)
    tcols = TILES // n_col
    places = BR * tcols
    spots = jnp.arange(places, dtype=jnp.int32)
    b_tiles, b_index, b_live = (
        lax.all_gather(matrix_tiles, ROW, axis=0, tiled=True),
        lax.all_gather(matrix_col, ROW, axis=0, tiled=True),
        lax.all_gather(matrix_live, ROW, axis=0, tiled=True),
    )
    flat_tiles = b_tiles.reshape(-1, tile, tile)
    half = slots_own // 2
    front_tiles, a_cell, a_count = (
        lax.all_gather(band_tiles[:, :half], COL, axis=1, tiled=True),
        lax.all_gather(band_cell, COL, axis=1, tiled=True),
        lax.all_gather(band_count, COL, axis=1, tiled=True),
    )
    counts = a_count[0]
    spill = jnp.maximum(counts - half, 0)
    before = jnp.cumsum(spill) - spill
    ending = before + spill
    mine = lax.axis_index(COL)
    own_before = jnp.take(before, mine)
    own_spill = jnp.maximum(band_count[0, 0] - half, 0)
    pack_spot = jnp.arange(half, dtype=jnp.int32)
    upper = jnp.arange(half, dtype=jnp.int32)
    place_w = (
        (pack_spot[:, None] == own_before + upper[None, :]) & (upper[None, :] < own_spill)
    ).astype(jnp.bfloat16)
    packed = jnp.einsum(
        "qs,sxy->qxy", place_w, band_tiles[0, half:], preferred_element_type=jnp.float32
    )
    spilled = (
        sum_by_parts(packed.astype(jnp.bfloat16), COL).astype(jnp.float32).astype(jnp.bfloat16)
    )
    holder = jnp.sum((ending[None, :] <= pack_spot[:, None]).astype(jnp.int32), axis=1)
    holder = jnp.clip(holder, 0, n_col - 1)
    spill_slot = jnp.clip(half + pack_spot - jnp.take(before, holder), 0, slots_own - 1)
    spill_cell = jnp.take(a_cell[0], holder * slots_own + spill_slot)
    spill_valid = pack_spot < jnp.sum(spill)
    front = jnp.arange(n_col * half, dtype=jnp.int32)
    front_source = front // half
    front_slot = front % half
    front_cell = jnp.take(a_cell[0], front_source * slots_own + front_slot)
    front_valid = front_slot < jnp.take(counts, front_source)
    sources = jnp.concatenate([front_source, holder])
    cells = jnp.concatenate([front_cell, spill_cell])
    valid = jnp.concatenate([front_valid, spill_valid])
    tiles = jnp.concatenate([front_tiles[0], spilled], axis=0)
    k_glob = sources * tcols + cells % tcols
    i_loc = cells // tcols
    picked = jnp.take(flat_tiles, k_glob, axis=0)
    picked_index = jnp.take(b_index.reshape(-1), k_glob)
    picked_live = jnp.take(b_live.reshape(-1), k_glob)
    live = (picked_live > 0) & valid
    position = i_loc * tcols + picked_index
    product = jnp.einsum("axy,ayz->axz", tiles, picked, preferred_element_type=jnp.float32)
    weights = ((position[:, None] == spots[None, :]) & live[:, None]).astype(jnp.float32)
    summed = jnp.einsum("ap,axz->pxz", weights, product, precision=lax.Precision.HIGHEST)
    own_live = jnp.arange(slots_own, dtype=jnp.int32) < band_count[0, 0]
    own_w = ((band_cell[0][:, None] == spots[None, :]) & own_live[:, None]).astype(jnp.bfloat16)
    base = jnp.einsum("sp,sxz->pxz", own_w, band_tiles[0], preferred_element_type=jnp.float32)
    expanded = jnp.minimum(1.0, base + summed)
    block = (
        expanded.reshape(BR, tcols, tile, tile)
        .transpose(0, 2, 1, 3)
        .reshape(BR * tile, tcols * tile)
    )
    total = over_axes(jnp.sum(expanded - base), ROW_COL)
    devices = lax.axis_size(ROW) * n_col
    gained = total / (tile * tile * devices * places)
    return (block.astype(jnp.bfloat16), gained)


def solution(mesh):
    split = Mesh(mesh.devices.reshape(4, 4, 4, 2), ("row_0", "row_1", "col_0", "col_1"))
    placed = (
        P(ROW, COL, None, None),
        P(ROW, COL),
        P(ROW, COL),
        P(ROW, COL, None, None),
        P(ROW, COL),
        P(ROW, COL),
    )
    return jax.shard_map(
        on_device, mesh=split, in_specs=placed, out_specs=(P(ROW, COL), P()), check_vma=False
    )
```

profile of v0, /device:TPU:1, one launch (start us, length us, event | category | flops | bytes accessed | tf_op | source)
XLA Modules:
  0.0 311.7 jit_solution(18201135137651149009)
XLA Ops:
  8.0 0.0 copy-start
  8.0 0.0 copy-start.2
  8.0 0.0 copy-start.3
  8.0 0.0 reduce-scatter.2.cloned.1.call-start
  8.9 1.2 dynamic-slice.3
  10.8 0.7 bitcast_dynamic-update-slice_fusion
  11.5 0.8 bitcast_dynamic-update-slice_fusion.1
  12.2 9.8 %all-reduce.2 = (s32[8]{0:T(128)S(1)}, s32[128]{0:T(128)S(1)}) all-reduce(s32[8]{0:T(128)S(1)} %bitcast_dynamic-update-slice_fusion, s32[128]{0:T(128)S(1)} %bitcast_dynamic-update-slice_fusion.1), channel_id=1, replica_groups=mesh['row_0'=4,'row_1'=4,'col_0'=4,'col_1'=2] {'col_0','col_1'}, use_global_device_ids=true, to_apply=%add.1 | all-reduce | flops 136 | bytes 1088
  22.0 0.6 fusion.42
  22.6 0.2 reduce-window.8
  22.8 0.6 dynamic-slice.2
  24.1 1.3 slice.7
  25.4 0.7 convolution_convert_fusion
  26.1 1.2 copy.24
  27.2 0.0 reduce-scatter.2.cloned.1.call-update
  27.3 0.0 all-gather.9.cloned.1.call-start
  27.3 0.5 all-gather.9.cloned.1.call-update
  27.8 0.0 all-gather.11.cloned.1.call-start
  27.9 29.4 %reduce-scatter.2.cloned.1.call-done = bf16[256,256]{1,0:T(8,128)(2,1)} async-done(((bf16[2048,256]{1,0:T(8,128)(2,1)}), bf16[256,256]{1,0:T(8,128)(2,1)}) %reduce-scatter.2.cloned.1.call-update) | async-done | bytes 131088 | tf_op jit(solution)/shard_map/reduce_scatter | solution.py:23
  57.3 0.0 all-gather.11.cloned.1.call-update
  57.3 0.0 all-gather.7.cloned.1.call-start
  57.4 0.0 copy-done
  57.4 1.0 slice.43
  58.4 0.0 all-gather.7.cloned.1.call-update
  58.4 0.1 convert_reduce_fusion
  58.6 0.6 gather_fusion.1
  59.3 0.6 gather_fusion.2
  59.9 0.8 gather_fusion
  60.7 0.0 copy-done.2
  60.7 17.2 %all-gather.1 = s32[16,1,8]{2,1,0:T(1,128)S(1)} all-gather(s32[1,1,8]{2,1,0:T(1,128)S(1)} %bitcast.102), channel_id=1, replica_groups=mesh['row_0'=4,'row_1'=4,'col_0'=4,'col_1'=2] {'row_0','row_1'}, dimensions={0}, use_global_device_ids=true | all-gather | bytes 544 | tf_op jit(solution)/shard_map/all_gather | solution.py:45
  77.9 0.5 broadcast.1065
  78.4 0.7 reduce.7
  79.1 0.1 reshape.382
  79.2 0.0 copy-done.3
  79.2 17.3 %all-gather.2 = s32[16,1,8]{2,1,0:T(1,128)S(1)} all-gather(s32[1,1,8]{2,1,0:T(1,128)S(1)} %bitcast.103), channel_id=1, replica_groups=mesh['row_0'=4,'row_1'=4,'col_0'=4,'col_1'=2] {'row_0','row_1'}, dimensions={0}, use_global_device_ids=true | all-gather | bytes 544 | tf_op jit(solution)/shard_map/all_gather | solution.py:46
  96.5 0.7 reduce.8
  97.1 0.1 reshape.383
  97.3 0.1 compare_and_fusion
  97.4 1.2 gather_fusion.4
  98.6 1.2 gather_fusion.5
  99.9 0.6 iota_compare_fusion.5
  100.4 0.1 fusion.37
  100.5 0.7 fusion.45
  101.2 5.0 %fusion.32 = pred[64]{0:T(512)(128)(4,1)S(1)} fusion(s32[]{:T(128)} %bitcast.20, s32[]{:T(128)} %bitcast.21, s32[]{:T(128)} %bitcast.22, s32[]{:T(128)} %bitcast.23, s32[]{:T(128)} %bitcast.24, s32[]{:T(128)} %bitcast.26, s32[]{:T(128)} %bitcast.25, s32[]{:T(128)} %bitcast.19), kind=kLoop, calls=%fused_computation.91 | loop fusion | flops 2880 | bytes 96 | tf_op jit(solution)/shard_map/lt | solution.py:82
  106.2 0.1 select_add_fusion
  106.3 0.1 add_and_fusion
  106.4 35.1 %all-gather.9.cloned.1.call-done = bf16[16,8,256,256]{3,2,1,0:T(8,128)(2,1)} async-done(((bf16[1,8,256,256]{3,2,1,0:T(8,128)(2,1)}), bf16[16,8,256,256]{3,2,1,0:T(8,128)(2,1)}) %all-gather.9.cloned.1.call-update) | async-done | bytes 16777232 | tf_op jit(solution)/shard_map/all_gather | solution.py:44
  141.5 11.8 %gather_fusion.3 = bf16[72,256,256]{2,1,0:T(8,128)(2,1)} fusion(bf16[128,256,256]{2,1,0:T(8,128)(2,1)} %bitcast.96, s32[1024]{0:T(1024)S(1)} %pad_clamp_fusion), kind=kCustom, calls=%fused_computation.5 | custom fusion | bytes 18874656 | tf_op jit(solution)/shard_map/jit(_take)/gather | solution.py:89
  153.3 13.3 %all-gather.11.cloned.1.call-done = bf16[2048,256]{1,0:T(8,128)(2,1)} async-done(((bf16[256,256]{1,0:T(8,128)(2,1)}), bf16[2048,256]{1,0:T(8,128)(2,1)}) %all-gather.11.cloned.1.call-update) | async-done | bytes 1048592 | tf_op jit(solution)/shard_map/all_gather | solution.py:26
  166.6 51.8 %all-gather.7.cloned.1.call-done = bf16[1,64,256,256]{3,2,0,1:T(8,128)(2,1)} async-done(((bf16[1,8,256,256]{3,2,0,1:T(8,128)(2,1)}), bf16[1,64,256,256]{3,2,0,1:T(8,128)(2,1)}) %all-gather.7.cloned.1.call-update) | async-done | bytes 8388624 | tf_op jit(solution)/shard_map/all_gather | solution.py:51
  218.4 13.5 %fusion.2 = f32[72,256,256]{2,1,0:T(8,128)} fusion(bf16[8,256,256]{2,1,0:T(8,128)(2,1)} %bitcast.105, bf16[64,256,256]{2,1,0:T(8,128)(2,1)} %bitcast.104, bf16[72,256,256]{2,1,0:T(8,128)(2,1)} %gather_fusion.3, pred[72]{0:T(512)(128)(4,1)S(1)} %get-tuple-element.16), kind=kOutput, calls=%fused_computation.8 | convolution fusion | flops 2425356288 | bytes 37748808 | tf_op jit(solution)/shard_map/axy,ayz->axz/dot_general | solution.py:94
  231.9 0.0 copy-start.1
  231.9 24.1 %fusion = f32[32,256,256]{2,0,1:T(8,128)S(1)} fusion(f32[72,256,256]{2,1,0:T(8,128)} %fusion.2, s32[72]{0:T(128)S(1)} %select_add_fusion, pred[72]{0:T(512)(128)(4,1)S(1)} %add_and_fusion), kind=kOutput, calls=%fused_computation.6 | convolution fusion | flops 1811943936 | bytes 27263336 | tf_op jit(solution)/shard_map/ap,axz->pxz/dot_general | solution.py:96
  256.0 0.0 copy-done.1
  256.0 5.2 %subtract_reduce_fusion = (f32[]{:T(128)}, bf16[32,256,256]{2,0,1:T(8,128)(2,1)}) fusion(f32[32,256,256]{2,0,1:T(8,128)S(1)} %fusion, bf16[16,256,256]{2,1,0:T(8,128)(2,1)S(1)} %bitcast.95, s32[16]{0:T(128)S(1)} %bitcast.101, pred[16]{0:T(512)(128)(4,1)S(1)} %iota_compare_fusion.6), kind=kOutput, calls=%fused_computation.14 | convolution fusion | flops 77595648 | bytes 14680148 | tf_op jit(solution)/shard_map/sp,sxz->pxz/dot_general | solution.py:99
  261.2 9.0 %psum.28 = f32[]{:T(128)} all-reduce(f32[]{:T(128)} %get-tuple-element.18), channel_id=1, replica_groups=mesh['row_0'=4,'row_1'=4,'col_0'=4,'col_1'=2] {'row_0'}, use_global_device_ids=true, to_apply=%region_5.7 | all-reduce | flops 1 | bytes 8 | tf_op jit(solution)/shard_map/psum | solution.py:32
  270.3 9.0 %psum.29 = f32[]{:T(128)} all-reduce(f32[]{:T(128)} %psum.28), channel_id=1, replica_groups=mesh['row_0'=4,'row_1'=4,'col_0'=4,'col_1'=2] {'row_1'}, use_global_device_ids=true, to_apply=%region_6.8 | all-reduce | flops 1 | bytes 8 | tf_op jit(solution)/shard_map/psum | solution.py:32
  279.3 7.1 %psum.30 = f32[]{:T(128)} all-reduce(f32[]{:T(128)} %psum.29), channel_id=1, replica_groups=mesh['row_0'=4,'row_1'=4,'col_0'=4,'col_1'=2] {'col_0'}, use_global_device_ids=true, to_apply=%region_7.9 | all-reduce | flops 1 | bytes 8 | tf_op jit(solution)/shard_map/psum | solution.py:32
  286.4 9.3 %psum.31 = f32[]{:T(128)} all-reduce(f32[]{:T(128)} %psum.30), channel_id=1, replica_groups=mesh['row_0'=4,'row_1'=4,'col_0'=4,'col_1'=2] {'col_1'}, use_global_device_ids=true, to_apply=%region_8.10 | all-reduce | flops 1 | bytes 8 | tf_op jit(solution)/shard_map/psum | solution.py:32
  295.6 2.5 copy.26
  298.1 4.2 %copy.28 = bf16[64,8,16,256]{3,1,2,0:T(8,128)(2,1)} copy(bf16[64,8,16,256]{3,2,1,0:T(8,128)(2,1)S(1)} %bitcast.93) | data formatting | bytes 8388608
  (19 shorter events, 0.1 us)
Async XLA Ops:
  8.0 49.4 %copy-start = (bf16[1,16,256,256]{3,2,1,0:T(8,128)(2,1)S(1)}, bf16[1,16,256,256]{3,2,1,0:T(8,128)(2,1)}, u32[]{:S(2)}) copy-start(bf16[1,16,256,256]{3,2,1,0:T(8,128)(2,1)} %param.8) | copy-start | bytes 6291460
  8.0 52.7 %copy-start.2 = (s32[1,8]{1,0:T(1,128)S(1)}, s32[1,8]{1,0:T(1,128)}, u32[]{:S(2)}) copy-start(s32[1,8]{1,0:T(1,128)} %param.12) | copy-start | bytes 100
  8.0 71.2 %copy-start.3 = (s32[1,8]{1,0:T(1,128)S(1)}, s32[1,8]{1,0:T(1,128)}, u32[]{:S(2)}) copy-start(s32[1,8]{1,0:T(1,128)} %param.13) | copy-start | bytes 100
  8.0 49.3 %reduce-scatter.2.cloned.1.call-start = ((), (), s32[]{:S(2)}) async-start(), calls=%async_computation.2 | async-start | bytes 1179648 | tf_op jit(solution)/shard_map/reduce_scatter | solution.py:23
  27.3 114.2 %all-gather.9.cloned.1.call-start = ((), (), s32[]{:S(2)}) async-start(), calls=%async_computation.3 | async-start | bytes 17825792 | tf_op jit(solution)/shard_map/all_gather | solution.py:44
  27.8 138.7 %all-gather.11.cloned.1.call-start = ((), (), s32[]{:S(2)}) async-start(), calls=%async_computation.4 | async-start | bytes 1179648 | tf_op jit(solution)/shard_map/all_gather | solution.py:26
  57.3 161.1 %all-gather.7.cloned.1.call-start = ((), (), s32[]{:S(2)}) async-start(), calls=%async_computation.1 | async-start | bytes 9437184 | tf_op jit(solution)/shard_map/all_gather | solution.py:51
  231.9 24.1 %copy-start.1 = (s32[1,16]{1,0:T(1,128)S(1)}, s32[1,16]{1,0:T(1,128)}, u32[]{:S(2)}) copy-start(s32[1,16]{1,0:T(1,128)} %param.9) | copy-start | bytes 196
Sparse Core Ops, SparseCore 0:
  27.4 29.8 reduce-scatter.1
Sparse Core Ops, SparseCore 1:
  29.9 111.5 all-gather.8
  143.1 23.5 all-gather.10
  168.8 49.6 all-gather.6
where the time goes:
time: 312 us
  waiting for transfers between devices  130 us (42%)
  blocking collectives  78.7 us (25%)
  matrix products  43.4 us (14%)
  local copies, waits for them, and re-layouts  31.2 us (10%)
  between operations  19.8 us (6%)
  other arithmetic  8.28 us (3%)
    all_gather x1, waiting for transfers between devices, on_device(): lax.all_gather(band_tiles[:, :half], COL, axis=1, tiled=True)  51.8 us
    all_gather x1, waiting for transfers between devices, on_device(): lax.all_gather(matrix_tiles, ROW, axis=0, tiled=True)  35.1 us
    psum x4, blocking collectives, over_axes(): shard = lax.psum(shard, axis)  34.4 us
    reduce_scatter x1, waiting for transfers between devices, sum_by_parts(): lax.psum_scatter(rows_for(lines, lax.axis_size(axis)), axis, scatter_dime...  29.4 us
    dot_general x1, matrix products, on_device(): jnp.einsum('ap,axz->pxz', weights, product, precision=lax.Precision.HIGHEST)  24.1 us
    all_gather x1, blocking collectives, on_device(): lax.all_gather(matrix_live, ROW, axis=0, tiled=True)  17.3 us
    all_gather x1, blocking collectives, on_device(): lax.all_gather(matrix_col, ROW, axis=0, tiled=True)  17.2 us
    dot_general x1, matrix products, on_device(): jnp.einsum('axy,ayz->axz', tiles, picked, preferred_element_type=jnp.floa...  13.5 us
  transfers between devices with their start and end apart: 4, of which 4 were waited for; matrix products, arithmetic and copies ran while one was open for 8% of the time, Pallas kernels for 0%

commit v1 on v0

--- a/solution.py
+++ b/solution.py
@@ -29,7 +29,7 @@
 
 def over_axes(shard, axes):
     for axis in axes:
-        shard = lax.psum(shard, axis)
+        shard = jnp.sum(lax.all_gather(shard, axis), axis=0)
     return shard
 
 

time: 312 us -> 323 us (1.035)
  local copies, waits for them, and re-layouts: 31.2 us -> 43.3 us
    psum x4 -> x0, blocking collectives: 34.4 us -> none  [over_axes(): shard = lax.psum(shard, axis)]
    unnamed x1 -> x5, blocking collectives: 9.78 us -> 41.4 us
    unnamed x13 -> x33, local copies, waits for them, and re-layouts: 6.91 us -> 17.1 us
where the time goes in v1:
time: 323 us; the launch traced here: 322 us
  waiting for transfers between devices  129 us (40%)
  blocking collectives  75.8 us (23%)
  matrix products  43.5 us (13%)
  local copies, waits for them, and re-layouts  43.3 us (13%)
  between operations  19.8 us (6%)
  other arithmetic  10.7 us (3%)
    all_gather x1, waiting for transfers between devices, on_device(): lax.all_gather(band_tiles[:, :half], COL, axis=1, tiled=True)  51.8 us
    unnamed x5, blocking collectives  41.4 us
    all_gather x1, waiting for transfers between devices, on_device(): lax.all_gather(matrix_tiles, ROW, axis=0, tiled=True)  34 us
    reduce_scatter x1, waiting for transfers between devices, sum_by_parts(): lax.psum_scatter(rows_for(lines, lax.axis_size(axis)), axis, scatter_dime...  29.4 us
    dot_general x1, matrix products, on_device(): jnp.einsum('ap,axz->pxz', weights, product, precision=lax.Precision.HIGHEST)  24.1 us
    all_gather x1, blocking collectives, on_device(): lax.all_gather(matrix_live, ROW, axis=0, tiled=True)  17.2 us
    all_gather x1, blocking collectives, on_device(): lax.all_gather(matrix_col, ROW, axis=0, tiled=True)  17.2 us
    unnamed x33, local copies, waits for them, and re-layouts  17.1 us
  transfers between devices with their start and end apart: 4, of which 4 were waited for; matrix products, arithmetic and copies ran while one was open for 8% of the time, Pallas kernels for 0%

profile of v1, /device:TPU:1, one launch (start us, length us, event | category | flops | bytes accessed | tf_op | source)
XLA Modules:
  0.0 322.4 jit_solution(7812773566089343894)
XLA Ops:
  8.1 0.0 reduce-scatter.2.cloned.1.call-start
  8.9 1.2 dynamic-slice.3
  10.8 0.7 bitcast_dynamic-update-slice_fusion
  11.5 0.8 bitcast_dynamic-update-slice_fusion.1
  12.2 9.8 %all-reduce.6 = (s32[8]{0:T(128)S(1)}, s32[128]{0:T(128)S(1)}) all-reduce(s32[8]{0:T(128)S(1)} %bitcast_dynamic-update-slice_fusion, s32[128]{0:T(128)S(1)} %bitcast_dynamic-update-slice_fusion.1), channel_id=1, replica_groups=mesh['row_0'=4,'row_1'=4,'col_0'=4,'col_1'=2] {'col_0','col_1'}, use_global_device_ids=true, to_apply=%add.1 | all-reduce | flops 136 | bytes 1088
  22.0 0.6 fusion.42
  22.6 0.2 reduce-window.8
  22.8 0.6 dynamic-slice.2
  24.1 1.3 slice.7
  25.4 0.7 convolution_convert_fusion
  26.1 1.2 copy.24
  27.3 0.0 all-gather.9.cloned.1.call-start
  27.3 0.5 all-gather.9.cloned.1.call-update
  27.9 0.0 all-gather.11.cloned.1.call-start
  27.9 29.4 %reduce-scatter.2.cloned.1.call-done = bf16[256,256]{1,0:T(8,128)(2,1)} async-done(((bf16[2048,256]{1,0:T(8,128)(2,1)}), bf16[256,256]{1,0:T(8,128)(2,1)}) %reduce-scatter.2.cloned.1.call-update) | async-done | bytes 131088 | tf_op jit(solution)/shard_map/reduce_scatter | solution.py:23
  57.3 0.0 all-gather.11.cloned.1.call-update
  57.3 0.0 all-gather.7.cloned.1.call-start
  57.4 1.0 slice.43
  58.5 0.0 all-gather.7.cloned.1.call-update
  58.5 0.1 convert_reduce_fusion
  58.6 0.6 gather_fusion.1
  59.3 0.6 gather_fusion.2
  60.0 0.8 gather_fusion
  60.7 17.2 %all-gather.1 = s32[16,1,8]{2,1,0:T(1,128)S(1)} all-gather(s32[1,1,8]{2,1,0:T(1,128)S(1)} %bitcast.110), channel_id=1, replica_groups=mesh['row_0'=4,'row_1'=4,'col_0'=4,'col_1'=2] {'row_0','row_1'}, dimensions={0}, use_global_device_ids=true | all-gather | bytes 544 | tf_op jit(solution)/shard_map/all_gather | solution.py:45
  77.9 0.5 broadcast.1069
  78.4 0.7 reduce.11
  79.1 0.1 reshape.382
  79.2 17.2 %all-gather.2 = s32[16,1,8]{2,1,0:T(1,128)S(1)} all-gather(s32[1,1,8]{2,1,0:T(1,128)S(1)} %bitcast.111), channel_id=1, replica_groups=mesh['row_0'=4,'row_1'=4,'col_0'=4,'col_1'=2] {'row_0','row_1'}, dimensions={0}, use_global_device_ids=true | all-gather | bytes 544 | tf_op jit(solution)/shard_map/all_gather | solution.py:46
  96.4 0.7 reduce.12
  97.1 0.1 reshape.383
  97.2 0.1 compare_and_fusion
  97.4 1.2 gather_fusion.4
  98.6 1.2 gather_fusion.5
  99.8 0.6 dynamic-slice.5
  100.4 0.6 dynamic-slice.6
  101.0 0.5 iota_compare_fusion.5
  101.6 0.1 fusion.37
  101.7 0.7 fusion.45
  102.3 5.0 %fusion.32 = pred[64]{0:T(512)(128)(4,1)S(1)} fusion(s32[]{:T(128)} %bitcast.20, s32[]{:T(128)} %bitcast.21, s32[]{:T(128)} %bitcast.22, s32[]{:T(128)} %bitcast.23, s32[]{:T(128)} %bitcast.24, s32[]{:T(128)} %bitcast.26, s32[]{:T(128)} %bitcast.25, s32[]{:T(128)} %bitcast.19), kind=kLoop, calls=%fused_computation.91 | loop fusion | flops 2880 | bytes 96 | tf_op jit(solution)/shard_map/lt | solution.py:82
  107.4 0.1 select_add_fusion
  107.5 0.1 add_and_fusion
  107.5 34.0 %all-gather.9.cloned.1.call-done = bf16[16,8,256,256]{3,2,1,0:T(8,128)(2,1)} async-done(((bf16[1,8,256,256]{3,2,1,0:T(8,128)(2,1)}), bf16[16,8,256,256]{3,2,1,0:T(8,128)(2,1)}) %all-gather.9.cloned.1.call-update) | async-done | bytes 16777232 | tf_op jit(solution)/shard_map/all_gather | solution.py:44
  141.5 11.8 %gather_fusion.3 = bf16[72,256,256]{2,1,0:T(8,128)(2,1)} fusion(bf16[128,256,256]{2,1,0:T(8,128)(2,1)} %bitcast.104, s32[1024]{0:T(1024)S(1)} %pad_clamp_fusion), kind=kCustom, calls=%fused_computation.5 | custom fusion | bytes 18874656 | tf_op jit(solution)/shard_map/jit(_take)/gather | solution.py:89
  153.3 13.3 %all-gather.11.cloned.1.call-done = bf16[2048,256]{1,0:T(8,128)(2,1)} async-done(((bf16[256,256]{1,0:T(8,128)(2,1)}), bf16[2048,256]{1,0:T(8,128)(2,1)}) %all-gather.11.cloned.1.call-update) | async-done | bytes 1048592 | tf_op jit(solution)/shard_map/all_gather | solution.py:26
  166.6 51.8 %all-gather.7.cloned.1.call-done = bf16[1,64,256,256]{3,2,0,1:T(8,128)(2,1)} async-done(((bf16[1,8,256,256]{3,2,0,1:T(8,128)(2,1)}), bf16[1,64,256,256]{3,2,0,1:T(8,128)(2,1)}) %all-gather.7.cloned.1.call-update) | async-done | bytes 8388624 | tf_op jit(solution)/shard_map/all_gather | solution.py:51
  218.5 13.5 %fusion.2 = f32[72,256,256]{2,1,0:T(8,128)} fusion(bf16[8,256,256]{2,1,0:T(8,128)(2,1)} %bitcast.113, bf16[64,256,256]{2,1,0:T(8,128)(2,1)} %bitcast.112, bf16[72,256,256]{2,1,0:T(8,128)(2,1)} %gather_fusion.3, pred[72]{0:T(512)(128)(4,1)S(1)} %get-tuple-element.16), kind=kOutput, calls=%fused_computation.8 | convolution fusion | flops 2425356288 | bytes 37748808 | tf_op jit(solution)/shard_map/axy,ayz->axz/dot_general | solution.py:94
  232.0 24.1 %fusion = f32[32,256,256]{2,0,1:T(8,128)S(1)} fusion(f32[72,256,256]{2,1,0:T(8,128)} %fusion.2, s32[72]{0:T(128)S(1)} %select_add_fusion, pred[72]{0:T(512)(128)(4,1)S(1)} %add_and_fusion), kind=kOutput, calls=%fused_computation.6 | convolution fusion | flops 1811943936 | bytes 27263336 | tf_op jit(solution)/shard_map/ap,axz->pxz/dot_general | solution.py:96
  256.1 5.2 %subtract_reduce_fusion = (f32[]{:T(128)}, bf16[32,256,256]{2,0,1:T(8,128)(2,1)}) fusion(f32[32,256,256]{2,0,1:T(8,128)S(1)} %fusion, bf16[16,256,256]{2,1,0:T(8,128)(2,1)S(1)} %bitcast.103, s32[16]{0:T(128)S(1)} %bitcast.109, pred[16]{0:T(512)(128)(4,1)S(1)} %iota_compare_fusion.6), kind=kOutput, calls=%fused_computation.14 | convolution fusion | flops 77595648 | bytes 14680148 | tf_op jit(solution)/shard_map/sp,sxz->pxz/dot_general | solution.py:99
  261.3 1.3 dynamic-update-slice.3
  262.6 0.7 dynamic-slice.7
  263.3 8.4 %all-reduce.2 = f32[4]{0:T(128)S(1)} all-reduce(f32[4]{0:T(128)S(1)} %dynamic-update-slice.3), channel_id=1, replica_groups=mesh['row_0'=4,'row_1'=4,'col_0'=4,'col_1'=2] {'row_0'}, use_global_device_ids=true, to_apply=%add.2 | all-reduce | flops 4 | bytes 32
  271.7 0.6 reduce_sum.66
  272.3 1.4 dynamic-update-slice.4
  273.7 0.6 dynamic-slice.8
  274.3 8.4 %all-reduce.3 = f32[4]{0:T(128)S(1)} all-reduce(f32[4]{0:T(128)S(1)} %dynamic-update-slice.4), channel_id=1, replica_groups=mesh['row_0'=4,'row_1'=4,'col_0'=4,'col_1'=2] {'row_1'}, use_global_device_ids=true, to_apply=%add.3 | all-reduce | flops 4 | bytes 32
  282.7 0.6 reduce_sum.67
  283.3 1.4 dynamic-update-slice.5
  284.7 4.4 %copy.26 = bf16[2,256,16,256]{3,2,1,0:T(8,128)(2,1)} copy(bf16[2,256,16,256]{3,2,0,1:T(8,128)(2,1)} %bitcast.100) | data formatting | bytes 8388608 | tf_op jit(solution)/shard_map/convert_element_type | solution.py:109
  289.2 6.4 %all-reduce.4 = f32[4]{0:T(128)S(1)} all-reduce(f32[4]{0:T(128)S(1)} %dynamic-update-slice.5), channel_id=1, replica_groups=mesh['row_0'=4,'row_1'=4,'col_0'=4,'col_1'=2] {'col_0'}, use_global_device_ids=true, to_apply=%add.4 | all-reduce | flops 4 | bytes 32
  295.6 0.6 reduce_sum.68
  296.2 1.4 dynamic-update-slice.6
  297.6 6.4 %copy.28 = bf16[64,8,16,256]{3,1,2,0:T(8,128)(2,1)} copy(bf16[64,8,16,256]{3,2,1,0:T(8,128)(2,1)} %bitcast.101) | data formatting | bytes 8388608
  304.0 8.4 %all-reduce.5 = f32[2]{0:T(128)S(1)} all-reduce(f32[2]{0:T(128)S(1)} %dynamic-update-slice.6), channel_id=1, replica_groups=mesh['row_0'=4,'row_1'=4,'col_0'=4,'col_1'=2] {'col_1'}, use_global_device_ids=true, to_apply=%add.5 | all-reduce | flops 2 | bytes 16
  312.4 0.6 reduce_sum.69
  (40 shorter events, 0.2 us)
Async XLA Ops:
  8.0 91.8 %copy-start.7 = (u32[128]{0:T(128)S(1)}, u32[128]{0:T(128)}, u32[]{:S(2)}) copy-start(u32[128]{0:T(128)} %constant.236) | copy-start | bytes 1540
  8.0 92.4 %copy-start.6 = (u32[128]{0:T(128)S(1)}, u32[128]{0:T(128)}, u32[]{:S(2)}) copy-start(u32[128]{0:T(128)} %constant.241) | copy-start | bytes 1540
  8.0 49.4 %copy-start = (bf16[1,16,256,256]{3,2,1,0:T(8,128)(2,1)S(1)}, bf16[1,16,256,256]{3,2,1,0:T(8,128)(2,1)}, u32[]{:S(2)}) copy-start(bf16[1,16,256,256]{3,2,1,0:T(8,128)(2,1)} %param.8) | copy-start | bytes 6291460
  8.0 52.7 %copy-start.2 = (s32[1,8]{1,0:T(1,128)S(1)}, s32[1,8]{1,0:T(1,128)}, u32[]{:S(2)}) copy-start(s32[1,8]{1,0:T(1,128)} %param.12) | copy-start | bytes 100
  8.0 71.2 %copy-start.3 = (s32[1,8]{1,0:T(1,128)S(1)}, s32[1,8]{1,0:T(1,128)}, u32[]{:S(2)}) copy-start(s32[1,8]{1,0:T(1,128)} %param.13) | copy-start | bytes 100
  8.1 49.3 %reduce-scatter.2.cloned.1.call-start = ((), (), s32[]{:S(2)}) async-start(), calls=%async_computation.2 | async-start | bytes 1179648 | tf_op jit(solution)/shard_map/reduce_scatter | solution.py:23
  27.3 114.2 %all-gather.9.cloned.1.call-start = ((), (), s32[]{:S(2)}) async-start(), calls=%async_computation.3 | async-start | bytes 17825792 | tf_op jit(solution)/shard_map/all_gather | solution.py:44
  27.9 138.7 %all-gather.11.cloned.1.call-start = ((), (), s32[]{:S(2)}) async-start(), calls=%async_computation.4 | async-start | bytes 1179648 | tf_op jit(solution)/shard_map/all_gather | solution.py:26
  57.3 161.1 %all-gather.7.cloned.1.call-start = ((), (), s32[]{:S(2)}) async-start(), calls=%async_computation.1 | async-start | bytes 9437184 | tf_op jit(solution)/shard_map/all_gather | solution.py:51
  232.0 24.1 %copy-start.1 = (s32[1,16]{1,0:T(1,128)S(1)}, s32[1,16]{1,0:T(1,128)}, u32[]{:S(2)}) copy-start(s32[1,16]{1,0:T(1,128)} %param.9) | copy-start | bytes 196
  256.1 6.6 %copy-start.5 = (u32[128]{0:T(128)S(1)}, u32[128]{0:T(128)}, u32[]{:S(2)}) copy-start(u32[128]{0:T(128)} %constant.246) | copy-start | bytes 1540
  256.1 17.7 %copy-start.4 = (u32[128]{0:T(128)S(1)}, u32[128]{0:T(128)}, u32[]{:S(2)}) copy-start(u32[128]{0:T(128)} %constant.251) | copy-start | bytes 1540
Sparse Core Ops, SparseCore 0:
  27.4 29.8 reduce-scatter.1
Sparse Core Ops, SparseCore 1:
  29.9 111.5 all-gather.8
  143.1 23.5 all-gather.10
  168.8 49.6 all-gather.6
